TPU v7x, 32 devices: a whole 2x2x4 slice. The times are simulated.
32 devices in a mesh: group: 4 (over y, core), dev: 8 (over z, x).
Axes of the slice: x: 2, y: 2, z: 4, core: 2. Of those that a mesh axis runs over, the one named last changes fastest.
Arguments:
- node_state: bfloat16 [16384, 512], P(('group', 'dev')), may hold values from -6 to 6
- hub_state: bfloat16 [64, 512], P('dev'), may hold values from -6 to 6
- w_edge_in: bfloat16 [512, 256], replicated, may hold values from -0.25 to 0.25
- w_edge_out: bfloat16 [256, 512], replicated, may hold values from -0.375 to 0.375
- w_update: bfloat16 [512, 512], replicated, may hold values from -0.25 to 0.25
- edge_src: int32 [131072], P(('group', 'dev')), may hold values from 0 to 319
- edge_dst: int32 [131072], P(('group', 'dev')), may hold values from 0 to 319
- edge_mask: int32 [131072], P(('group', 'dev')), may hold values 0 or 1
- send_list: int32 [32, 8, 32], P(('group', 'dev')), may hold values from 0 to 511
- send_count: int32 [32, 8], P(('group', 'dev')), may hold values from 8 to 32, as said below
- node_cot: bfloat16 [16384, 512], P(('group', 'dev')), may hold values from -0.059814453 to 0.059814453
- hub_cot: bfloat16 [64, 512], P('dev'), may hold values from -0.059814453 to 0.059814453
Outputs:
- new_state: bfloat16 [16384, 512], P(('group', 'dev'))
- new_hub: bfloat16 [64, 512], P('dev')
- grad_in: float32 [512, 256], replicated
- grad_out: float32 [256, 512], replicated
- grad_update: float32 [512, 512], replicated
Inputs may be any that keep to these rules, and one draw needn't show every extreme that they name: Device 0 sends 32 live slots to peer 0: send_count[0, 0] = 32.
All inputs are finite; a program needn't handle non-finite values. No bound on the sum of `edge_mask` on one device may be relied on, other than what follows from the above.
Results may differ from a plain program's by a relative error of at most 0.0064.
The roundings to bfloat16 on the way count: a program that leaves them out, or rounds other values in their place, can miss the bound.
Values may be sent and summed in bfloat16 or wider, within the bound.
No kernel may reach another device: no remote copies, remote signals or barrier semaphores. Data moves between devices by JAX's collectives and lax.ppermute only.
A program may use at most 64 MiB of HBM per device.

v0:
```python
import jax
import jax.numpy as jnp
from jax import lax
from jax.sharding import PartitionSpec as P


def silu_grad(values):
    sigmoid_v = jax.nn.sigmoid(values)
    return sigmoid_v * (1.0 + values * (1.0 - sigmoid_v))


def finish(states, summed, degree, w_update):
    mean_part = summed / jnp.maximum(degree, 1.0)[:, None]
    mixed_rows = (states.astype(jnp.float32) + mean_part).astype(jnp.bfloat16)
    pre_update = jnp.dot(mixed_rows, w_update, preferred_element_type=jnp.float32)
    updated = (states.astype(jnp.float32) + jax.nn.silu(pre_update)).astype(jnp.bfloat16)
    return (mixed_rows, pre_update, updated)


def backward_rows(cotangent, pre_update, degree, w_update):
    grad_pre = (cotangent.astype(jnp.float32) * silu_grad(pre_update)).astype(jnp.bfloat16)
    grad_mix = jnp.dot(grad_pre, w_update.T, preferred_element_type=jnp.float32)
    grad_sum = (grad_mix / jnp.maximum(degree, 1.0)[:, None]).astype(jnp.bfloat16)
    return (grad_pre, grad_sum)


def shards(
    node_state,
    hub_state,
    w_edge_in,
    w_edge_out,
    w_update,
    edge_src,
    edge_dst,
    edge_mask,
    send_list,
    send_count,
    node_cot,
    hub_cot,
):
    width = node_state.shape[1]
    master_rows = node_state.shape[0]
    send_rows = send_list[0]
    peer_total = send_rows.shape[0]
    slot_width = send_rows.shape[1]
    mirror_total = peer_total * slot_width
    live_slot = jnp.arange(slot_width)[None, :] < send_count[0][:, None]
    flat_rows = send_rows.reshape(-1)
    flat_live = live_slot.reshape(-1)
    selector = (
        (flat_rows[:, None] == jnp.arange(master_rows)[None, :]) & flat_live[:, None]
    ).astype(jnp.bfloat16)
    contract = (((0,), (0,)), ((), ()))
    outgoing = jnp.dot(selector, node_state, preferred_element_type=jnp.float32).astype(
        jnp.bfloat16
    )
    mirror_rows = lax.all_to_all(
        outgoing.reshape(peer_total, slot_width, width),
        "dev",
        split_axis=0,
        concat_axis=0,
        tiled=True,
    )
    hub_table = lax.all_gather(hub_state, "dev", axis=0, tiled=True)
    local_table = jnp.concatenate([mirror_rows.reshape(mirror_total, width), hub_table], axis=0)
    local_rows = local_table.shape[0]
    edge_total = edge_src.shape[0]
    block_size = min(1024, edge_total)
    block_count = edge_total // block_size
    sources = edge_src.reshape(block_count, block_size)
    targets = edge_dst.reshape(block_count, block_size)
    edge_keep = edge_mask.reshape(block_count, block_size)
    row_ids = jnp.arange(local_rows)[None, :]

    def forward_step(totals, pieces):
        source_ids, target_ids, keep_ids = pieces
        gathered = local_table[source_ids]
        pre_act = jnp.dot(gathered, w_edge_in, preferred_element_type=jnp.float32)
        hidden = jax.nn.silu(pre_act).astype(jnp.bfloat16)
        message = jnp.dot(hidden, w_edge_out, preferred_element_type=jnp.float32).astype(
            jnp.bfloat16
        )
        onehot = ((target_ids[:, None] == row_ids) & (keep_ids[:, None] > 0)).astype(jnp.bfloat16)
        added = lax.dot_general(onehot, message, contract, preferred_element_type=jnp.float32)
        tally = jnp.sum(onehot, axis=0, dtype=jnp.float32)
        return ((totals[0] + added, totals[1] + tally), pre_act)

    start_fwd = (jnp.zeros((local_rows, width), jnp.float32), jnp.zeros((local_rows,), jnp.float32))
    (partial_value, counts_local), saved_acts = lax.scan(
        forward_step, start_fwd, (sources, targets, edge_keep)
    )
    mirror_part = (
        partial_value[:mirror_total].reshape(peer_total, slot_width, width).astype(jnp.bfloat16)
    )
    mirror_count = counts_local[:mirror_total].reshape(peer_total, slot_width).astype(jnp.bfloat16)
    back_part, back_count = (
        lax.all_to_all(mirror_part, "dev", split_axis=0, concat_axis=0, tiled=True),
        lax.all_to_all(mirror_count, "dev", split_axis=0, concat_axis=0, tiled=True),
    )
    summed = lax.dot_general(
        selector,
        back_part.reshape(mirror_total, width),
        contract,
        preferred_element_type=jnp.float32,
    )
    degree = lax.dot_general(
        selector, back_count.reshape(mirror_total, 1), contract, preferred_element_type=jnp.float32
    )[:, 0]
    hub_part = partial_value[mirror_total:]
    hub_count = counts_local[mirror_total:]
    whole_part, whole_count = (
        lax.psum(hub_part.astype(jnp.bfloat16), "group").astype(jnp.float32),
        lax.psum(hub_count.astype(jnp.bfloat16), "group").astype(jnp.float32),
    )
    hub_summed, hub_degree = (
        lax.psum_scatter(
            whole_part.astype(jnp.bfloat16), "dev", scatter_dimension=0, tiled=True
        ).astype(jnp.float32),
        lax.psum_scatter(
            whole_count.astype(jnp.bfloat16), "dev", scatter_dimension=0, tiled=True
        ).astype(jnp.float32),
    )
    mixed_rows, pre_update, new_state = finish(node_state, summed, degree, w_update)
    hub_mixed, hub_pre, new_hub = finish(hub_state, hub_summed, hub_degree, w_update)
    grad_pre, grad_sum = backward_rows(node_cot, pre_update, degree, w_update)
    hub_grad_pre, hub_grad_sum = backward_rows(hub_cot, hub_pre, hub_degree, w_update)
    grad_outgoing = jnp.dot(selector, grad_sum, preferred_element_type=jnp.float32).astype(
        jnp.bfloat16
    )
    grad_mirror = lax.all_to_all(
        grad_outgoing.reshape(peer_total, slot_width, width),
        "dev",
        split_axis=0,
        concat_axis=0,
        tiled=True,
    )
    grad_hubs = lax.all_gather(hub_grad_sum, "dev", axis=0, tiled=True)
    grad_table = jnp.concatenate([grad_mirror.reshape(mirror_total, width), grad_hubs], axis=0)
    hub_weight = (lax.axis_index("group") == 0).astype(jnp.float32)
    grad_update = lax.dot_general(
        mixed_rows, grad_pre, contract, preferred_element_type=jnp.float32
    )
    grad_update = grad_update + hub_weight * lax.dot_general(
        hub_mixed, hub_grad_pre, contract, preferred_element_type=jnp.float32
    )

    def backward_step(totals, pieces):
        source_ids, target_ids, keep_ids, pre_act = pieces
        gathered = local_table[source_ids]
        hidden = jax.nn.silu(pre_act).astype(jnp.bfloat16)
        grad_message = jnp.where(
            keep_ids[:, None] > 0, grad_table[target_ids], jnp.zeros((), jnp.bfloat16)
        )
        grad_w_out = lax.dot_general(
            hidden, grad_message, contract, preferred_element_type=jnp.float32
        )
        grad_hidden = jnp.dot(grad_message, w_edge_out.T, preferred_element_type=jnp.float32)
        grad_act = (grad_hidden * silu_grad(pre_act)).astype(jnp.bfloat16)
        grad_w_in = lax.dot_general(
            gathered, grad_act, contract, preferred_element_type=jnp.float32
        )
        return ((totals[0] + grad_w_in, totals[1] + grad_w_out), None)

    start = (jnp.zeros(w_edge_in.shape, jnp.float32), jnp.zeros(w_edge_out.shape, jnp.float32))
    local_grads, _ = lax.scan(backward_step, start, (sources, targets, edge_keep, saved_acts))
    grad_in, grad_out, grad_upd = lax.psum(
        (local_grads[0], local_grads[1], grad_update), ("group", "dev")
    )
    return (new_state, new_hub, grad_in, grad_out, grad_upd)


def solution(mesh):
    return jax.shard_map(
        shards,
        mesh=mesh,
        in_specs=(
            P(("group", "dev"), None),
            P("dev", None),
            P(),
            P(),
            P(),
            P(("group", "dev")),
            P(("group", "dev")),
            P(("group", "dev")),
            P(("group", "dev"), None, None),
            P(("group", "dev"), None),
            P(("group", "dev"), None),
            P("dev", None),
        ),
        out_specs=(P(("group", "dev"), None), P("dev", None), P(), P(), P()),
        check_vma=False,
    )
```

profile of v0, /device:TPU:0, one launch (start us, length us, event | category | flops | bytes accessed | tf_op | source)
XLA Modules:
  0.0 417.0 jit_solution(8544541724577750692)
XLA Ops:
  10.9 7.2 %all-to-all-start = ((bf16[8,32,512]{2,1,0:T(8,128)(2,1)}), bf16[8,32,512]{2,1,0:T(8,128)(2,1)S(1)}, u32[]{:S(2)}, u32[]{:S(2)}) async-start(bf16[8,32,512]{2,1,0:T(8,128)(2,1)} %bitcast.1), calls=%async_computation | async-start | bytes 524288 | tf_op jit(solution)/shard_map/all_to_all | solution.py:57
  20.4 31.2 %all_gather.6 = bf16[64,512]{1,0:T(8,128)(2,1)S(1)} all-gather(bf16[8,512]{1,0:T(8,128)(2,1)} %param.17), channel_id=1, replica_groups=mesh['group'=4,'dev'=8] {'dev'}, dimensions={0}, use_global_device_ids=true | all-gather | bytes 73728 | tf_op jit(solution)/shard_map/all_gather | solution.py:64
  51.7 33.4 %while.28 = (s32[]{:T(128)}, f32[320,512]{1,0:T(8,128)}, f32[320]{0:T(512)S(1)}, f32[4,1024,256]{2,1,0:T(8,128)}, s32[4,1024]{1,0:T(4,128)S(1)}, /*index=5*/s32[...) while((s32[]{:T(128)}, f32[320,512]{1,0:T(8,128)}, ...), condition=%wide.region_2.3_spmd.clone, body=%wide.region_0.2_spmd.clone.sunk | while | flops 876877120 | bytes 10273476 | solution.py:89
  51.8 4.0 gather_fusion
  59.3 4.0 gather_fusion
  67.9 4.0 gather_fusion
  76.5 4.0 gather_fusion
  85.8 5.4 %all-to-all-start.2 = ((bf16[8,1,32]{2,1,0:T(2,128)(2,1)}), bf16[8,1,32]{2,1,0:T(2,128)(2,1)S(1)}, u32[]{:S(2)}, u32[]{:S(2)}) async-start(bf16[8,1,32]{2,1,0:T(2,128)(2,1)} %convert_element_type.118), calls=%async_computation.2 | async-start | bytes 8192 | tf_op jit(solution)/shard_map/all_to_all | solution.py:98
  95.1 21.8 %all-reduce = bf16[64]{0:T(256)(128)(2,1)S(1)} all-reduce(bf16[64]{0:T(256)(128)(2,1)S(1)} %slice.27), channel_id=3, replica_groups=mesh['group'=4,'dev'=8] {'dev'}, use_global_device_ids=true, to_apply=%region_6.7.clone | all-reduce | flops 64 | bytes 256
  120.8 38.2 %reduce-scatter.2.cloned.1.call-done = bf16[8,512]{1,0:T(8,128)(2,1)} async-done(((bf16[64,512]{1,0:T(8,128)(2,1)}), bf16[8,512]{1,0:T(8,128)(2,1)}) %reduce-scatter.2.cloned.1.call-update) | async-done | bytes 8208 | tf_op jit(solution)/shard_map/reduce_scatter | solution.py:116
  159.0 6.0 %all-reduce.2 = (bf16[8,512]{1,0:T(8,128)(2,1)S(1)}, bf16[8]{0:T(256)(128)(2,1)S(1)}) all-reduce(bf16[8,512]{1,0:T(8,128)(2,1)} %reduce-scatter.2.cloned.1.call-done, bf16[8]{0:T(256)(128)(2,1)S(1)} %dynamic-slice.1), channel_id=1, replica_groups=mesh['group'=4,'dev'=8] {'group'}, use_global_device_ids=true, to_apply=%region_3.4 | all-reduce | flops 4104 | bytes 16416 | tf_op jit(solution)/shard_map/psum | solution.py:112
  166.1 30.5 %all_gather.7 = bf16[64,512]{1,0:T(8,128)(2,1)S(1)} all-gather(bf16[8,512]{1,0:T(8,128)(2,1)S(1)} %fusion.42), channel_id=1, replica_groups=mesh['group'=4,'dev'=8] {'dev'}, dimensions={0}, use_global_device_ids=true | all-gather | bytes 73728 | tf_op jit(solution)/shard_map/all_gather | solution.py:137
  202.3 3.6 all-to-all-start.3
  207.8 6.3 %all-to-all-done.3 = bf16[8,32,512]{2,1,0:T(8,128)(2,1)S(1)} async-done(((bf16[8,32,512]{2,1,0:T(8,128)(2,1)}), bf16[8,32,512]{2,1,0:T(8,128)(2,1)S(1)}, u32[]{:S(2)}, u32[]{:S(2)}) %all-to-all-start.3) | async-done | bytes 262176 | tf_op jit(solution)/shard_map/all_to_all | solution.py:130
  214.1 56.7 %while.29 = (s32[]{:T(128)}, f32[512,256]{1,0:T(8,128)}, f32[256,512]{1,0:T(8,128)}, s32[4,1024]{1,0:T(4,128)S(1)}, bf16[320,512]{1,0:T(8,128)(2,1)S(1)}, /*inde...) while((s32[]{:T(128)}, f32[512,256]{1,0:T(8,128)}, ...), condition=%wide.region_8.9_spmd.clone, body=%wide.region_7.8_spmd.clone.sunk | while | flops 810558464 | bytes 11845768 | solution.py:165
  214.2 4.0 gather_fusion.2
  218.2 4.0 gather_fusion.1
  228.1 4.0 gather_fusion.2
  232.1 4.0 gather_fusion.1
  242.4 4.0 gather_fusion.2
  246.3 4.0 gather_fusion.1
  256.6 4.0 gather_fusion.2
  260.6 4.0 gather_fusion.1
  270.8 133.3 %all-reduce.5.cloned.1.call-done = (f32[512,256]{1,0:T(8,128)}, f32[256,512]{1,0:T(8,128)}, f32[512,512]{1,0:T(8,128)}) async-done(((f32[512,256]{1,0:T(8,128)}, f32[256,512]{1,0:T(8,128)}, f32[512,512]{1,0:T(8,128)}), (f32[512,256]{1,0:T(8,128)}, f32[256,512]{1,0:T(8,128)}, f32[512,512]{1,0:T(8,128)})) %all-reduce.5.cloned.1.call-update) | async-done | bytes 2097168 | tf_op jit(solution)/shard_map/psum | solution.py:166
  (128 shorter events, 70.4 us)
Async XLA Ops:
  7.2 157.8 %copy-start = (bf16[512,512]{1,0:T(8,128)(2,1)S(1)}, bf16[512,512]{1,0:T(8,128)(2,1)}, u32[]{:S(2)}) copy-start(bf16[512,512]{1,0:T(8,128)(2,1)} %param.20) | copy-start | bytes 1572868
  10.9 40.7 %all-to-all-start = ((bf16[8,32,512]{2,1,0:T(8,128)(2,1)}), bf16[8,32,512]{2,1,0:T(8,128)(2,1)S(1)}, u32[]{:S(2)}, u32[]{:S(2)}) async-start(bf16[8,32,512]{2,1,0:T(8,128)(2,1)} %bitcast.1), calls=%async_computation | async-start | bytes 524288 | tf_op jit(solution)/shard_map/all_to_all | solution.py:57
  51.7 39.6 %copy-start.6 = (u32[32]{0:T(128)S(1)}, u32[32]{0:T(128)}, u32[]{:S(2)}) copy-start(u32[32]{0:T(128)} %constant.65) | copy-start | bytes 388
  51.7 113.3 %copy-start.2 = (bf16[8,512]{1,0:T(8,128)(2,1)S(1)}, bf16[8,512]{1,0:T(8,128)(2,1)}, u32[]{:S(2)}) copy-start(bf16[8,512]{1,0:T(8,128)(2,1)} %param.17) | copy-start | bytes 24580
  51.7 114.2 %copy-start.3 = (bf16[8,512]{1,0:T(8,128)(2,1)S(1)}, bf16[8,512]{1,0:T(8,128)(2,1)}, u32[]{:S(2)}) copy-start(bf16[8,512]{1,0:T(8,128)(2,1)} %param.27) | copy-start | bytes 24580
  51.7 4.0 copy-start.1
  51.8 5.5 %copy-start.5 = (bf16[256,512]{1,0:T(8,128)(2,1)S(1)}, bf16[256,512]{1,0:T(8,128)(2,1)}, u32[]{:S(2)}) copy-start(bf16[256,512]{1,0:T(8,128)(2,1)} %get-tuple-element.406) | copy-start | bytes 786436 | tf_op jit(solution)/shard_map/while
  59.2 4.0 copy-start.1
  59.3 5.5 %copy-start.5 = (bf16[256,512]{1,0:T(8,128)(2,1)S(1)}, bf16[256,512]{1,0:T(8,128)(2,1)}, u32[]{:S(2)}) copy-start(bf16[256,512]{1,0:T(8,128)(2,1)} %get-tuple-element.406) | copy-start | bytes 786436 | tf_op jit(solution)/shard_map/while
  67.9 4.0 copy-start.1
  67.9 5.5 %copy-start.5 = (bf16[256,512]{1,0:T(8,128)(2,1)S(1)}, bf16[256,512]{1,0:T(8,128)(2,1)}, u32[]{:S(2)}) copy-start(bf16[256,512]{1,0:T(8,128)(2,1)} %get-tuple-element.406) | copy-start | bytes 786436 | tf_op jit(solution)/shard_map/while
  76.5 4.0 copy-start.1
  76.5 5.5 %copy-start.5 = (bf16[256,512]{1,0:T(8,128)(2,1)S(1)}, bf16[256,512]{1,0:T(8,128)(2,1)}, u32[]{:S(2)}) copy-start(bf16[256,512]{1,0:T(8,128)(2,1)} %get-tuple-element.406) | copy-start | bytes 786436 | tf_op jit(solution)/shard_map/while
  85.8 31.2 %all-to-all-start.2 = ((bf16[8,1,32]{2,1,0:T(2,128)(2,1)}), bf16[8,1,32]{2,1,0:T(2,128)(2,1)S(1)}, u32[]{:S(2)}, u32[]{:S(2)}) async-start(bf16[8,1,32]{2,1,0:T(2,128)(2,1)} %convert_element_type.118), calls=%async_computation.2 | async-start | bytes 8192 | tf_op jit(solution)/shard_map/all_to_all | solution.py:98
  91.2 67.8 %reduce-scatter.2.cloned.1.call-start = ((), (), s32[]{:S(2)}) async-start(), calls=%async_computation.5 | async-start | bytes 73728 | tf_op jit(solution)/shard_map/reduce_scatter | solution.py:116
  92.5 105.6 %copy-start.4 = (bf16[512,512]{1,0:T(8,128)(2,1)S(1)}, bf16[512,512]{1,0:T(8,128)(2,1)}, u32[]{:S(2)}) copy-start(bf16[512,512]{1,0:T(8,128)(2,1)} %param.26) | copy-start | bytes 1572868
  117.0 79.6 %all-to-all-start.1 = ((bf16[8,32,512]{2,1,0:T(8,128)(2,1)}), bf16[8,32,512]{2,1,0:T(8,128)(2,1)S(1)}, u32[]{:S(2)}, u32[]{:S(2)}) async-start(bf16[8,32,512]{2,1,0:T(8,128)(2,1)} %bitcast.3), calls=%async_computation.1 | async-start | bytes 524288 | tf_op jit(solution)/shard_map/all_to_all | solution.py:97
  202.3 11.8 %all-to-all-start.3 = ((bf16[8,32,512]{2,1,0:T(8,128)(2,1)}), bf16[8,32,512]{2,1,0:T(8,128)(2,1)S(1)}, u32[]{:S(2)}, u32[]{:S(2)}) async-start(bf16[8,32,512]{2,1,0:T(8,128)(2,1)} %bitcast.6), calls=%async_computation.3 | async-start | bytes 524288 | tf_op jit(solution)/shard_map/all_to_all | solution.py:130
  205.9 198.3 %all-reduce.5.cloned.1.call-start = ((), (), s32[]{:S(2)}) async-start(), calls=%async_computation.6 | async-start | bytes 4194304 | tf_op jit(solution)/shard_map/psum | solution.py:166
Sparse Core Ops, SparseCore 0:
  96.0 62.9 reduce-scatter.1
  270.9 133.1 all-reduce.4
where the time goes:
time: 418 us; the launch traced here: 417 us
  waiting for transfers between devices  178 us (43%)
  blocking collectives  89.5 us (21%)
  local copies, waits for them, and re-layouts  59.5 us (14%)
  matrix products  51.1 us (12%)
  starting transfers between devices  19.8 us (5%)
  between operations  14.9 us (4%)
    psum x1, waiting for transfers between devices, shards(): lax.psum((local_grads[0], local_grads[1], grad_update), ('group', 'dev'))  133 us
    reduce_scatter x1, waiting for transfers between devices, shards(): lax.psum_scatter(whole_part.astype(jnp.bfloat16), 'dev', scatter_dimensio...  38.2 us
    all_gather x1, blocking collectives, shards(): hub_table = lax.all_gather(hub_state, 'dev', axis=0, tiled=True)  31.2 us
    all_gather x1, blocking collectives, shards(): grad_hubs = lax.all_gather(hub_grad_sum, 'dev', axis=0, tiled=True)  30.5 us
    unnamed x1, blocking collectives  21.8 us
    gather x4, local copies, waits for them, and re-layouts, backward_step(): grad_table[target_ids]  15.9 us
    gather x4, local copies, waits for them, and re-layouts, backward_step(): gathered = local_table[source_ids]  15.9 us
    gather x4, local copies, waits for them, and re-layouts, forward_step(): gathered = local_table[source_ids]  15.9 us
  transfers between devices with their start and end apart: 6, of which 3 were waited for; matrix products, arithmetic and copies ran while one was open for 2% of the time, Pallas kernels for 0%

commit v1 on v0

--- a/solution.py
+++ b/solution.py
@@ -164,7 +164,7 @@
     start = (jnp.zeros(w_edge_in.shape, jnp.float32), jnp.zeros(w_edge_out.shape, jnp.float32))
     local_grads, _ = lax.scan(backward_step, start, (sources, targets, edge_keep, saved_acts))
     grad_in, grad_out, grad_upd = lax.psum(
-        (local_grads[0], local_grads[1], grad_update), ("group", "dev")
+        lax.psum((local_grads[0], local_grads[1], grad_update), "dev"), "group"
     )
     return (new_state, new_hub, grad_in, grad_out, grad_upd)
 

time: 418 us -> 440 us (1.053)
  waiting for transfers between devices: 178 us -> 200 us
    psum x1 -> x2, waiting for transfers between devices: 133 us -> 155 us  [the longest x1 102 us: shards(): lax.psum((local_grads[0], local_grads[1], grad_update), 'dev')]
  transfers between devices with their start and end apart: 6 -> 7, of which waited for: 3 -> 4; matrix products, arithmetic and copies ran while one was open for 2% -> 2% of each run, Pallas kernels for 0% -> 0%
where the time goes in v1:
time: 440 us; the launch traced here: 439 us
  waiting for transfers between devices  200 us (45%)
  blocking collectives  89.5 us (20%)
  local copies, waits for them, and re-layouts  59.5 us (14%)
  matrix products  51.1 us (12%)
  starting transfers between devices  19.8 us (4%)
  between operations  14.6 us (3%)
    psum x1, waiting for transfers between devices, shards(): lax.psum((local_grads[0], local_grads[1], grad_update), 'dev')  102 us
    psum x1, waiting for transfers between devices, shards(): lax.psum(lax.psum((local_grads[0], local_grads[1], grad_update), 'dev'),...  53.4 us
    reduce_scatter x1, waiting for transfers between devices, shards(): lax.psum_scatter(whole_part.astype(jnp.bfloat16), 'dev', scatter_dimensio...  38.2 us
    all_gather x1, blocking collectives, shards(): hub_table = lax.all_gather(hub_state, 'dev', axis=0, tiled=True)  31.2 us
    all_gather x1, blocking collectives, shards(): grad_hubs = lax.all_gather(hub_grad_sum, 'dev', axis=0, tiled=True)  30.5 us
    unnamed x1, blocking collectives  21.8 us
    gather x4, local copies, waits for them, and re-layouts, forward_step(): gathered = local_table[source_ids]  15.9 us
    gather x4, local copies, waits for them, and re-layouts, backward_step(): grad_table[target_ids]  15.9 us
  transfers between devices with their start and end apart: 7, of which 4 were waited for; matrix products, arithmetic and copies ran while one was open for 2% of the time, Pallas kernels for 0%

profile of v1, /device:TPU:0, one launch (start us, length us, event | category | flops | bytes accessed | tf_op | source)
XLA Modules:
  0.0 438.7 jit_solution(2264708601854535573)
XLA Ops:
  10.9 7.2 %all-to-all-start = ((bf16[8,32,512]{2,1,0:T(8,128)(2,1)}), bf16[8,32,512]{2,1,0:T(8,128)(2,1)S(1)}, u32[]{:S(2)}, u32[]{:S(2)}) async-start(bf16[8,32,512]{2,1,0:T(8,128)(2,1)} %bitcast.1), calls=%async_computation | async-start | bytes 524288 | tf_op jit(solution)/shard_map/all_to_all | solution.py:57
  20.4 31.2 %all_gather.6 = bf16[64,512]{1,0:T(8,128)(2,1)S(1)} all-gather(bf16[8,512]{1,0:T(8,128)(2,1)} %param.17), channel_id=1, replica_groups=mesh['group'=4,'dev'=8] {'dev'}, dimensions={0}, use_global_device_ids=true | all-gather | bytes 73728 | tf_op jit(solution)/shard_map/all_gather | solution.py:64
  51.7 33.4 %while.28 = (s32[]{:T(128)}, f32[320,512]{1,0:T(8,128)}, f32[320]{0:T(512)S(1)}, f32[4,1024,256]{2,1,0:T(8,128)}, s32[4,1024]{1,0:T(4,128)S(1)}, /*index=5*/s32[...) while((s32[]{:T(128)}, f32[320,512]{1,0:T(8,128)}, ...), condition=%wide.region_2.3_spmd.clone, body=%wide.region_0.2_spmd.clone.sunk | while | flops 876877120 | bytes 10273476 | solution.py:89
  51.8 4.0 gather_fusion
  59.3 4.0 gather_fusion
  67.9 4.0 gather_fusion
  76.5 4.0 gather_fusion
  85.7 5.4 %all-to-all-start.2 = ((bf16[8,1,32]{2,1,0:T(2,128)(2,1)}), bf16[8,1,32]{2,1,0:T(2,128)(2,1)S(1)}, u32[]{:S(2)}, u32[]{:S(2)}) async-start(bf16[8,1,32]{2,1,0:T(2,128)(2,1)} %convert_element_type.118), calls=%async_computation.2 | async-start | bytes 8192 | tf_op jit(solution)/shard_map/all_to_all | solution.py:98
  95.1 21.8 %all-reduce = bf16[64]{0:T(256)(128)(2,1)S(1)} all-reduce(bf16[64]{0:T(256)(128)(2,1)S(1)} %slice.27), channel_id=3, replica_groups=mesh['group'=4,'dev'=8] {'dev'}, use_global_device_ids=true, to_apply=%region_6.7.clone | all-reduce | flops 64 | bytes 256
  120.8 38.2 %reduce-scatter.2.cloned.1.call-done = bf16[8,512]{1,0:T(8,128)(2,1)} async-done(((bf16[64,512]{1,0:T(8,128)(2,1)}), bf16[8,512]{1,0:T(8,128)(2,1)}) %reduce-scatter.2.cloned.1.call-update) | async-done | bytes 8208 | tf_op jit(solution)/shard_map/reduce_scatter | solution.py:116
  158.9 6.0 %all-reduce.3 = (bf16[8,512]{1,0:T(8,128)(2,1)S(1)}, bf16[8]{0:T(256)(128)(2,1)S(1)}) all-reduce(bf16[8,512]{1,0:T(8,128)(2,1)} %reduce-scatter.2.cloned.1.call-done, bf16[8]{0:T(256)(128)(2,1)S(1)} %dynamic-slice.1), channel_id=1, replica_groups=mesh['group'=4,'dev'=8] {'group'}, use_global_device_ids=true, to_apply=%region_3.4 | all-reduce | flops 4104 | bytes 16416 | tf_op jit(solution)/shard_map/psum | solution.py:112
  166.0 30.5 %all_gather.7 = bf16[64,512]{1,0:T(8,128)(2,1)S(1)} all-gather(bf16[8,512]{1,0:T(8,128)(2,1)S(1)} %fusion.42), channel_id=1, replica_groups=mesh['group'=4,'dev'=8] {'dev'}, dimensions={0}, use_global_device_ids=true | all-gather | bytes 73728 | tf_op jit(solution)/shard_map/all_gather | solution.py:137
  207.7 6.3 %all-to-all-done.3 = bf16[8,32,512]{2,1,0:T(8,128)(2,1)S(1)} async-done(((bf16[8,32,512]{2,1,0:T(8,128)(2,1)}), bf16[8,32,512]{2,1,0:T(8,128)(2,1)S(1)}, u32[]{:S(2)}, u32[]{:S(2)}) %all-to-all-start.3) | async-done | bytes 262176 | tf_op jit(solution)/shard_map/all_to_all | solution.py:130
  214.1 56.7 %while.29 = (s32[]{:T(128)}, f32[512,256]{1,0:T(8,128)}, f32[256,512]{1,0:T(8,128)}, s32[4,1024]{1,0:T(4,128)S(1)}, bf16[320,512]{1,0:T(8,128)(2,1)S(1)}, /*inde...) while((s32[]{:T(128)}, f32[512,256]{1,0:T(8,128)}, ...), condition=%wide.region_8.9_spmd.clone, body=%wide.region_7.8_spmd.clone.sunk | while | flops 810558464 | bytes 11845768 | solution.py:165
  214.1 4.0 gather_fusion.2
  218.1 4.0 gather_fusion.1
  228.1 4.0 gather_fusion.2
  232.1 4.0 gather_fusion.1
  242.3 4.0 gather_fusion.2
  246.3 4.0 gather_fusion.1
  256.5 4.0 gather_fusion.2
  260.5 4.0 gather_fusion.1
  270.8 102.0 %all-reduce.7.cloned.1.call-done = (f32[512,256]{1,0:T(8,128)}, f32[256,512]{1,0:T(8,128)}, f32[512,512]{1,0:T(8,128)}) async-done(((f32[512,256]{1,0:T(8,128)}, f32[256,512]{1,0:T(8,128)}, f32[512,512]{1,0:T(8,128)}), (f32[512,256]{1,0:T(8,128)}, f32[256,512]{1,0:T(8,128)}, f32[512,512]{1,0:T(8,128)})) %all-reduce.7.cloned.1.call-update) | async-done | bytes 2097168 | tf_op jit(solution)/shard_map/psum | solution.py:167
  372.9 53.4 %all-reduce.9.cloned.1.call-done = (f32[512,256]{1,0:T(8,128)}, f32[256,512]{1,0:T(8,128)}, f32[512,512]{1,0:T(8,128)}) async-done(((f32[512,256]{1,0:T(8,128)}, f32[256,512]{1,0:T(8,128)}, f32[512,512]{1,0:T(8,128)}), (f32[512,256]{1,0:T(8,128)}, f32[256,512]{1,0:T(8,128)}, f32[512,512]{1,0:T(8,128)})) %all-reduce.9.cloned.1.call-update) | async-done | bytes 2097168 | tf_op jit(solution)/shard_map/psum | solution.py:166
  (131 shorter events, 74.0 us)
Async XLA Ops:
  7.2 157.8 %copy-start = (bf16[512,512]{1,0:T(8,128)(2,1)S(1)}, bf16[512,512]{1,0:T(8,128)(2,1)}, u32[]{:S(2)}) copy-start(bf16[512,512]{1,0:T(8,128)(2,1)} %param.20) | copy-start | bytes 1572868
  10.9 40.7 %all-to-all-start = ((bf16[8,32,512]{2,1,0:T(8,128)(2,1)}), bf16[8,32,512]{2,1,0:T(8,128)(2,1)S(1)}, u32[]{:S(2)}, u32[]{:S(2)}) async-start(bf16[8,32,512]{2,1,0:T(8,128)(2,1)} %bitcast.1), calls=%async_computation | async-start | bytes 524288 | tf_op jit(solution)/shard_map/all_to_all | solution.py:57
  51.7 39.6 %copy-start.6 = (u32[32]{0:T(128)S(1)}, u32[32]{0:T(128)}, u32[]{:S(2)}) copy-start(u32[32]{0:T(128)} %constant.65) | copy-start | bytes 388
  51.7 113.3 %copy-start.2 = (bf16[8,512]{1,0:T(8,128)(2,1)S(1)}, bf16[8,512]{1,0:T(8,128)(2,1)}, u32[]{:S(2)}) copy-start(bf16[8,512]{1,0:T(8,128)(2,1)} %param.17) | copy-start | bytes 24580
  51.7 114.1 %copy-start.3 = (bf16[8,512]{1,0:T(8,128)(2,1)S(1)}, bf16[8,512]{1,0:T(8,128)(2,1)}, u32[]{:S(2)}) copy-start(bf16[8,512]{1,0:T(8,128)(2,1)} %param.27) | copy-start | bytes 24580
  51.7 4.0 copy-start.1
  51.8 5.4 %copy-start.5 = (bf16[256,512]{1,0:T(8,128)(2,1)S(1)}, bf16[256,512]{1,0:T(8,128)(2,1)}, u32[]{:S(2)}) copy-start(bf16[256,512]{1,0:T(8,128)(2,1)} %get-tuple-element.409) | copy-start | bytes 786436 | tf_op jit(solution)/shard_map/while
  59.2 4.0 copy-start.1
  59.3 5.5 %copy-start.5 = (bf16[256,512]{1,0:T(8,128)(2,1)S(1)}, bf16[256,512]{1,0:T(8,128)(2,1)}, u32[]{:S(2)}) copy-start(bf16[256,512]{1,0:T(8,128)(2,1)} %get-tuple-element.409) | copy-start | bytes 786436 | tf_op jit(solution)/shard_map/while
  67.9 4.0 copy-start.1
  67.9 5.5 %copy-start.5 = (bf16[256,512]{1,0:T(8,128)(2,1)S(1)}, bf16[256,512]{1,0:T(8,128)(2,1)}, u32[]{:S(2)}) copy-start(bf16[256,512]{1,0:T(8,128)(2,1)} %get-tuple-element.409) | copy-start | bytes 786436 | tf_op jit(solution)/shard_map/while
  76.5 4.0 copy-start.1
  76.5 5.5 %copy-start.5 = (bf16[256,512]{1,0:T(8,128)(2,1)S(1)}, bf16[256,512]{1,0:T(8,128)(2,1)}, u32[]{:S(2)}) copy-start(bf16[256,512]{1,0:T(8,128)(2,1)} %get-tuple-element.409) | copy-start | bytes 786436 | tf_op jit(solution)/shard_map/while
  85.7 31.2 %all-to-all-start.2 = ((bf16[8,1,32]{2,1,0:T(2,128)(2,1)}), bf16[8,1,32]{2,1,0:T(2,128)(2,1)S(1)}, u32[]{:S(2)}, u32[]{:S(2)}) async-start(bf16[8,1,32]{2,1,0:T(2,128)(2,1)} %convert_element_type.118), calls=%async_computation.2 | async-start | bytes 8192 | tf_op jit(solution)/shard_map/all_to_all | solution.py:98
  91.2 67.8 %reduce-scatter.2.cloned.1.call-start = ((), (), s32[]{:S(2)}) async-start(), calls=%async_computation.5 | async-start | bytes 73728 | tf_op jit(solution)/shard_map/reduce_scatter | solution.py:116
  92.5 105.6 %copy-start.4 = (bf16[512,512]{1,0:T(8,128)(2,1)S(1)}, bf16[512,512]{1,0:T(8,128)(2,1)}, u32[]{:S(2)}) copy-start(bf16[512,512]{1,0:T(8,128)(2,1)} %param.26) | copy-start | bytes 1572868
  117.0 79.6 %all-to-all-start.1 = ((bf16[8,32,512]{2,1,0:T(8,128)(2,1)}), bf16[8,32,512]{2,1,0:T(8,128)(2,1)S(1)}, u32[]{:S(2)}, u32[]{:S(2)}) async-start(bf16[8,32,512]{2,1,0:T(8,128)(2,1)} %bitcast.3), calls=%async_computation.1 | async-start | bytes 524288 | tf_op jit(solution)/shard_map/all_to_all | solution.py:97
  202.2 11.8 %all-to-all-start.3 = ((bf16[8,32,512]{2,1,0:T(8,128)(2,1)}), bf16[8,32,512]{2,1,0:T(8,128)(2,1)S(1)}, u32[]{:S(2)}, u32[]{:S(2)}) async-start(bf16[8,32,512]{2,1,0:T(8,128)(2,1)} %bitcast.6), calls=%async_computation.3 | async-start | bytes 524288 | tf_op jit(solution)/shard_map/all_to_all | solution.py:130
  205.8 167.0 %all-reduce.7.cloned.1.call-start = ((), (), s32[]{:S(2)}) async-start(), calls=%async_computation.6 | async-start | bytes 4194304 | tf_op jit(solution)/shard_map/psum | solution.py:167
  270.8 155.5 %all-reduce.9.cloned.1.call-start = ((), (), s32[]{:S(2)}) async-start(), calls=%async_computation.7 | async-start | bytes 4194304 | tf_op jit(solution)/shard_map/psum | solution.py:166
Sparse Core Ops, SparseCore 0:
  96.0 62.9 reduce-scatter.1
  270.9 101.9 all-reduce.6
  375.4 50.8 all-reduce.8
